TPU v7x, 32 devices: a whole 2x2x4 slice. The times are simulated.
32 devices in a mesh: ctx: 16 (over z, y, core), exp: 2 (over x).
Axes of the slice: x: 2, y: 2, z: 4, core: 2. Of those that a mesh axis runs over, the one named last changes fastest.
Arguments:
- queries: bfloat16 [256, 16, 128], P(('exp', 'ctx')), may hold values from -6 to 6
- key_heads: bfloat16 [256, 8, 128], P('ctx', 'exp'), may hold values from -6 to 6
- value_heads: bfloat16 [256, 8, 128], P('ctx', 'exp'), may hold values from -6 to 6
- expert_ids: int32 [256, 16], P(('exp', 'ctx')), may hold values from 0 to 63, all different within a row; in each aligned block of 8 rows (0 to 7, 8 to 15, ...) at most 3 rows name the same one
- gate_logits: float32 [256, 16], P(('exp', 'ctx')), may hold values from -4 to 4
- out_weight: bfloat16 [64, 128, 8192], P('exp', None, 'ctx'), may hold values from -0.5 to 0.5
Outputs:
- mixed_out: bfloat16 [256, 8192], P('exp', 'ctx')
Inputs may be any that keep to these rules, and one draw needn't show every extreme that they name: `expert_ids`: each token names 16 different experts; among the 8 tokens of an aligned block no expert is named by more than 3 tokens, a bound that some block reaches.
All inputs are finite; a program needn't handle non-finite values.
Results may differ from a plain program's by a relative error of at most 0.018.
Values may be sent and summed in bfloat16 or wider, within the bound.
A program may use at most 64 MiB of HBM per device.

v0:
```python
import jax
import jax.numpy as jnp
from jax import lax
from jax.sharding import PartitionSpec as P

EXPERTS = 64
HD = 128
TOP = 16
MOST = 3


NEG_FLOOR = -1e30


def attend_block(running, key_block, value_block, key_start, query_heads, query_pos):
    row_max, row_sum, weighted = running
    scores = jnp.einsum(
        "hrd,khd->hrk", query_heads, key_block, preferred_element_type=jnp.float32
    ) * HD ** (-0.5)
    key_pos = key_start + jnp.arange(key_block.shape[0], dtype=jnp.int32)
    visible = key_pos[None, None, :] <= query_pos[:, :, None]
    scores = jnp.where(visible, scores, NEG_FLOOR)
    new_max = jnp.maximum(row_max, jnp.max(scores, axis=2))
    exponents = jnp.where(visible, jnp.exp(scores - new_max[:, :, None]), 0.0)
    rescale = jnp.exp(row_max - new_max)
    row_sum = row_sum * rescale + jnp.sum(exponents, axis=2)
    weighted = weighted * rescale[:, :, None] + jnp.einsum(
        "hrk,khd->hrd",
        exponents.astype(jnp.bfloat16),
        value_block,
        preferred_element_type=jnp.float32,
    )
    return (new_max, row_sum, weighted)


def attend_piece(running, key_piece, value_piece, query_heads, query_pos, shard_len):
    total_rows = key_piece.shape[0]
    shard_count = total_rows // shard_len
    limit = max(1024, shard_len)
    per_block = 1
    for candidate in range(1, shard_count + 1):
        if shard_count % candidate == 0 and candidate * shard_len <= limit:
            per_block = candidate
    block_width = per_block * shard_len

    def step_block(block_num, carried):
        key_block = lax.dynamic_slice_in_dim(key_piece, block_num * block_width, block_width, 0)
        value_block = lax.dynamic_slice_in_dim(value_piece, block_num * block_width, block_width, 0)
        return attend_block(
            carried, key_block, value_block, block_num * block_width, query_heads, query_pos
        )

    return lax.fori_loop(0, total_rows // block_width, step_block, running)


def body(queries, key_heads, value_heads, expert_ids, gate_logits, out_weight):
    ctx_count = lax.axis_size("ctx")
    exp_count = lax.axis_size("exp")
    ctx_index = lax.axis_index("ctx")
    exp_index = lax.axis_index("exp")
    tok_dev = queries.shape[0]
    span_len = key_heads.shape[0]
    heads_dev = key_heads.shape[1]
    per_device = EXPERTS // exp_count
    group_size = per_device // heads_dev
    group_rows = group_size * MOST
    row_total = tok_dev * TOP
    block_first = (exp_index * ctx_count + ctx_index) * tok_dev
    col_width = out_weight.shape[2]
    gate_exp = jnp.exp(gate_logits)
    gate_values = (gate_exp / jnp.sum(gate_exp, axis=1, keepdims=True)).astype(jnp.bfloat16)
    flat_ids = expert_ids.reshape(row_total)
    one_hot = (flat_ids[:, None] == jnp.arange(EXPERTS, dtype=jnp.int32)[None, :]).astype(jnp.int32)
    earlier = jnp.cumsum(one_hot, axis=0) - one_hot
    row_rank = jnp.sum(earlier * one_hot, axis=1)
    slot_id = flat_ids * MOST + row_rank
    placed = jnp.arange(EXPERTS * MOST, dtype=jnp.int32)[:, None] == slot_id[None, :]
    send_rows = jnp.dot(
        placed.astype(jnp.bfloat16),
        queries.reshape(row_total, HD),
        preferred_element_type=jnp.float32,
    ).astype(jnp.bfloat16)
    token_pos = block_first + jnp.arange(row_total, dtype=jnp.int32) // TOP
    send_pos = jnp.sum(jnp.where(placed, token_pos[None, :], 0), axis=1)
    send_gate = jnp.sum(
        jnp.where(placed, gate_values.reshape(row_total).astype(jnp.float32)[None, :], 0.0), axis=1
    ).astype(jnp.bfloat16)
    layout = (exp_count, heads_dev, group_rows)
    recv_rows, recv_pos, recv_gate = (
        lax.all_to_all(
            send_rows.reshape(layout + (HD,)), "exp", split_axis=0, concat_axis=2, tiled=True
        ),
        lax.all_to_all(send_pos.reshape(layout), "exp", split_axis=0, concat_axis=2, tiled=True),
        lax.all_to_all(send_gate.reshape(layout), "exp", split_axis=0, concat_axis=2, tiled=True),
    )
    query_heads = recv_rows.reshape(heads_dev, exp_count * group_rows, HD)
    query_pos = recv_pos.reshape(heads_dev, exp_count * group_rows)
    row_gate = recv_gate.reshape(heads_dev, exp_count * group_rows)
    initial = (
        jnp.full(query_pos.shape, NEG_FLOOR, jnp.float32),
        jnp.zeros(query_pos.shape, jnp.float32),
        jnp.zeros(query_heads.shape, jnp.float32),
    )
    finished = attend_piece(
        initial,
        lax.all_gather(key_heads, "ctx", axis=0, tiled=True),
        lax.all_gather(value_heads, "ctx", axis=0, tiled=True),
        query_heads,
        query_pos,
        span_len,
    )
    row_max, row_sum, weighted = finished
    gated_rows = (
        row_gate.astype(jnp.float32)[:, :, None] * (weighted / row_sum[:, :, None])
    ).astype(jnp.bfloat16)
    gated_grid = gated_rows.reshape(1, heads_dev, exp_count, group_size, MOST, HD)
    pos_grid = query_pos.reshape(1, heads_dev, exp_count, group_size, MOST)
    src_ids = jnp.arange(exp_count, dtype=jnp.int32)
    weight_grid = out_weight.reshape(heads_dev, group_size, HD, col_width)
    gated_piece, pos_piece = lax.all_gather((gated_grid, pos_grid), "ctx", axis=0, tiled=True)
    shards = gated_piece.shape[0]
    projected = jnp.einsum(
        "chsgmd,hgdo->chsgmo", gated_piece, weight_grid, preferred_element_type=jnp.float32
    )
    ctx_ids = jnp.arange(shards, dtype=jnp.int32)
    block_start = (
        src_ids[None, None, :, None, None] * ctx_count + ctx_ids[:, None, None, None, None]
    ) * tok_dev
    local_pos = jnp.clip(pos_piece - block_start, 0, tok_dev - 1)
    segment = (
        src_ids[None, None, :, None, None] * (shards * tok_dev)
        + jnp.arange(shards, dtype=jnp.int32)[:, None, None, None, None] * tok_dev
        + local_pos
    )
    summed = jax.ops.segment_sum(
        projected.reshape(-1, projected.shape[-1]),
        segment.reshape(-1),
        num_segments=exp_count * shards * tok_dev,
    )
    partial_term = summed.reshape(exp_count, shards * tok_dev, projected.shape[-1])
    partial_term = partial_term.reshape(exp_count * ctx_count * tok_dev, partial_term.shape[-1])
    mixed_out = lax.psum_scatter(
        partial_term.astype(jnp.bfloat16), "exp", scatter_dimension=0, tiled=True
    )
    return mixed_out


def solution(mesh):
    in_specs = (
        P(("exp", "ctx"), None, None),
        P("ctx", "exp", None),
        P("ctx", "exp", None),
        P(("exp", "ctx"), None),
        P(("exp", "ctx"), None),
        P("exp", None, "ctx"),
    )
    out_specs = P("exp", "ctx")
    return jax.shard_map(body, mesh=mesh, in_specs=in_specs, out_specs=out_specs, check_vma=False)
```

profile of v0, /device:TPU:0, one launch (start us, length us, event | category | flops | bytes accessed | tf_op | source)
XLA Modules:
  0.0 169.8 jit_solution(10358233354645093596)
XLA Ops:
  6.5 0.8 reshape.160
  7.4 0.2 reduce_window_sum.11
  7.6 0.2 select_reduce_fusion.2
  7.8 0.8 exponential_reduce_fusion
  8.6 0.8 fusion.15
  9.4 0.1 select_reduce_fusion
  9.5 0.7 convert_element_type.58
  10.2 4.2 %all-to-all-start.1 = ((bf16[2,4,24]{2,1,0:T(4,128)(2,1)}), bf16[2,4,24]{2,1,0:T(4,128)(2,1)S(1)}, u32[]{:S(2)}, u32[]{:S(2)}) async-start(bf16[2,4,24]{2,1,0:T(4,128)(2,1)} %convert_element_type.58), calls=%async_computation.1 | async-start | bytes 4096 | tf_op jit(solution)/shard_map/all_to_all | solution.py:94
  14.4 0.8 convolution_convert_fusion
  15.2 0.7 copy.45
  15.9 22.8 %all_gather.13 = bf16[256,4,128]{2,0,1:T(8,128)(2,1)S(1)} all-gather(bf16[16,4,128]{2,0,1:T(8,128)(2,1)S(1)} %copy.45), channel_id=1, replica_groups=mesh['ctx'=16,'exp'=2] {'ctx'}, dimensions={0}, use_global_device_ids=true | all-gather | bytes 278528 | tf_op jit(solution)/shard_map/all_gather | solution.py:106
  38.7 0.7 copy.46
  39.5 18.1 %all_gather.14 = bf16[256,4,128]{2,0,1:T(8,128)(2,1)S(1)} all-gather(bf16[16,4,128]{2,0,1:T(8,128)(2,1)S(1)} %copy.46), channel_id=1, replica_groups=mesh['ctx'=16,'exp'=2] {'ctx'}, dimensions={0}, use_global_device_ids=true | all-gather | bytes 278528 | tf_op jit(solution)/shard_map/all_gather | solution.py:107
  57.8 0.7 reshape.161
  58.5 3.2 %all-to-all-start = ((s32[2,4,24]{2,1,0:T(4,128)}), s32[2,4,24]{2,1,0:T(4,128)S(1)}, u32[]{:S(2)}, u32[]{:S(2)}) async-start(s32[2,4,24]{2,1,0:T(4,128)} %reshape.161), calls=%async_computation | async-start | bytes 8192 | tf_op jit(solution)/shard_map/all_to_all | solution.py:93
  61.8 3.7 %all-to-all-done = s32[2,4,24]{2,1,0:T(4,128)S(1)} async-done(((s32[2,4,24]{2,1,0:T(4,128)}), s32[2,4,24]{2,1,0:T(4,128)S(1)}, u32[]{:S(2)}, u32[]{:S(2)}) %all-to-all-start) | async-done | bytes 800 | tf_op jit(solution)/shard_map/all_to_all | solution.py:93
  65.5 3.3 %all-to-all-start.2 = ((bf16[2,4,24,128]{3,2,1,0:T(8,128)(2,1)}), bf16[2,4,24,128]{3,2,1,0:T(8,128)(2,1)S(1)}, u32[]{:S(2)}, u32[]{:S(2)}) async-start(bf16[2,4,24,128]{3,2,1,0:T(8,128)(2,1)} %bitcast.6), calls=%async_computation.2 | async-start | bytes 98304 | tf_op jit(solution)/shard_map/all_to_all | solution.py:90
  68.9 0.1 copy.40
  69.0 19.3 %all_gather.12 = s32[16,4,2,8,3]{3,1,4,2,0:T(4,128)S(1)} all-gather(s32[1,4,2,8,3]{3,1,4,2,0:T(4,128)S(1)} %copy.40), channel_id=1, replica_groups=mesh['ctx'=16,'exp'=2] {'ctx'}, dimensions={0}, use_global_device_ids=true | all-gather | bytes 13056 | tf_op jit(solution)/shard_map/all_gather | solution.py:120
  88.3 0.1 clamp_add_fusion
  88.6 0.8 copy.41
  89.4 0.3 reshape.173
  89.7 0.3 fusion.19
  90.0 0.2 fusion.7
  90.2 0.2 fusion.3
  90.5 19.8 %all_gather.15 = bf16[16,4,2,8,3,128]{5,3,4,2,1,0:T(8,128)(2,1)S(1)} all-gather(bf16[1,4,2,8,3,128]{5,3,4,2,1,0:T(8,128)(2,1)S(1)} %copy.48), channel_id=1, replica_groups=mesh['ctx'=16,'exp'=2] {'ctx'}, dimensions={0}, use_global_device_ids=true | all-gather | bytes 835584 | tf_op jit(solution)/shard_map/all_gather | solution.py:120
  110.3 3.4 %convolution_bitcast_fusion = f32[16,4,2,8,3,512]{5,0,4,2,3,1:T(8,128)S(1)} fusion(bf16[4,8,128,512,1,1]{3,2,5,4,1,0:T(8,128)(2,1)} %bitcast.32, bf16[16,4,2,8,3,128]{5,3,4,2,1,0:T(8,128)(2,1)S(1)} %all_gather.15), kind=kOutput, calls=%fused_computation.1 | convolution fusion | flops 402653184 | bytes 11272192 | tf_op jit(solution)/shard_map/chsgmd,hgdo->chsgmo/dot_general | solution.py:122
  113.7 7.5 %copy.50 = f32[16,4,2,8,3,512]{5,4,3,2,1,0:T(4,128)} copy(f32[16,4,2,8,3,512]{5,0,4,2,3,1:T(8,128)S(1)} %convolution_bitcast_fusion) | data formatting | bytes 12582912 | tf_op jit(solution)/shard_map/chsgmd,hgdo->chsgmo/transpose | solution.py:122
  121.3 10.8 %reshape.175 = f32[3072,512]{1,0:T(8,128)} reshape(f32[16,4,2,8,3,512]{5,4,3,2,1,0:T(4,128)} %copy.50) | data formatting | bytes 12582912 | tf_op jit(solution)/shard_map/reshape | solution.py:136
  132.0 19.3 %scatter_custom_fusion = f32[256,512]{1,0:T(8,128)S(1)} fusion(s32[3072]{0:T(1024)S(1)} %reshape.173, f32[3072,512]{1,0:T(8,128)} %reshape.175, f32[]{:T(128)} %constant.27.clone.1), kind=kCustom, calls=%fused_computation.10 | custom fusion | flops 1572864 | bytes 524800 | tf_op jit(solution)/shard_map/scatter-add | solution.py:135
  151.4 0.7 convert_element_type.66
  152.1 10.9 %reduce-scatter.2.cloned.1.call-done = bf16[128,512]{1,0:T(8,128)(2,1)} async-done(((bf16[256,512]{1,0:T(8,128)(2,1)}), bf16[128,512]{1,0:T(8,128)(2,1)}) %reduce-scatter.2.cloned.1.call-update) | async-done | bytes 131088 | tf_op jit(solution)/shard_map/reduce_scatter | solution.py:142
  (25 shorter events, 0.7 us)
Async XLA Ops:
  6.5 7.9 %copy-start = (bf16[8,16,128]{2,1,0:T(8,128)(2,1)S(1)}, bf16[8,16,128]{2,1,0:T(8,128)(2,1)}, u32[]{:S(2)}) copy-start(bf16[8,16,128]{2,1,0:T(8,128)(2,1)} %param.6) | copy-start | bytes 98308
  10.2 48.2 %all-to-all-start.1 = ((bf16[2,4,24]{2,1,0:T(4,128)(2,1)}), bf16[2,4,24]{2,1,0:T(4,128)(2,1)S(1)}, u32[]{:S(2)}, u32[]{:S(2)}) async-start(bf16[2,4,24]{2,1,0:T(4,128)(2,1)} %convert_element_type.58), calls=%async_computation.1 | async-start | bytes 4096 | tf_op jit(solution)/shard_map/all_to_all | solution.py:94
  58.5 7.0 %all-to-all-start = ((s32[2,4,24]{2,1,0:T(4,128)}), s32[2,4,24]{2,1,0:T(4,128)S(1)}, u32[]{:S(2)}, u32[]{:S(2)}) async-start(s32[2,4,24]{2,1,0:T(4,128)} %reshape.161), calls=%async_computation | async-start | bytes 8192 | tf_op jit(solution)/shard_map/all_to_all | solution.py:93
  65.5 24.2 %all-to-all-start.2 = ((bf16[2,4,24,128]{3,2,1,0:T(8,128)(2,1)}), bf16[2,4,24,128]{3,2,1,0:T(8,128)(2,1)S(1)}, u32[]{:S(2)}, u32[]{:S(2)}) async-start(bf16[2,4,24,128]{3,2,1,0:T(8,128)(2,1)} %bitcast.6), calls=%async_computation.2 | async-start | bytes 98304 | tf_op jit(solution)/shard_map/all_to_all | solution.py:90
  68.8 94.2 %reduce-scatter.2.cloned.1.call-start = ((), (), s32[]{:S(2)}) async-start(), calls=%async_computation.4 | async-start | bytes 393216 | tf_op jit(solution)/shard_map/reduce_scatter | solution.py:142
Sparse Core Ops, SparseCore 0:
  152.2 10.6 reduce-scatter.1
where the time goes:
time: 171 us; the launch traced here: 170 us
  blocking collectives  80 us (47%)
  local copies, waits for them, and re-layouts  23.5 us (14%)
  other arithmetic  22.7 us (13%)
  waiting for transfers between devices  14.6 us (9%)
  between operations  13.5 us (8%)
  starting transfers between devices  10.8 us (6%)
  matrix products  4.73 us (3%)
    all_gather x2, blocking collectives, body(): lax.all_gather((gated_grid, pos_grid), 'ctx', axis=0, tiled=True)  39.1 us
    all_gather x1, blocking collectives, body(): lax.all_gather(key_heads, 'ctx', axis=0, tiled=True)  22.8 us
    scatter-add x1, other arithmetic, body(): jax.ops.segment_sum(projected.reshape(-1, projected.shape[-1]), segment.r...  19.3 us
    all_gather x1, blocking collectives, body(): lax.all_gather(value_heads, 'ctx', axis=0, tiled=True)  18.1 us
    reduce_scatter x1, waiting for transfers between devices, body(): lax.psum_scatter(partial_term.astype(jnp.bfloat16), 'exp', scatter_dimens...  10.9 us
    reshape x1, local copies, waits for them, and re-layouts, body(): projected.reshape(-1, projected.shape[-1])  10.8 us
    transpose x1, local copies, waits for them, and re-layouts, body(): jnp.einsum('chsgmd,hgdo->chsgmo', gated_piece, weight_grid, preferred_ele...  7.54 us
    all_to_all x1, starting transfers between devices, body(): lax.all_to_all(send_gate.reshape(layout), 'exp', split_axis=0, concat_axi...  4.21 us
  transfers between devices with their start and end apart: 4, of which 2 were waited for; matrix products, arithmetic and copies ran while one was open for 3% of the time, Pallas kernels for 0%

commit v1 on v0

v1 whole, which is shorter than its diff:
```python
import functools

import jax
import jax.numpy as jnp
from jax import lax
from jax.experimental import pallas as pl
from jax.experimental.pallas import tpu as pltpu
from jax.sharding import PartitionSpec as P

EXPERTS = 64
MOST = 3
LANES = 128
META_ROWS = 16
F32 = jnp.float32
BF16 = jnp.bfloat16
MESH = pl.DeviceIdType.MESH


def iota(shape, dim):
    return lax.broadcasted_iota(jnp.int32, shape, dim)


def flood(buf, send, recv, coords, n, use):
    slow, mid, last, slows = coords
    me = (slow * 2 + mid) * 2 + last
    mid_peer = (slow * 2 + (1 - mid)) * 2 + last
    last_peer = (slow * 2 + mid) * 2 + (1 - last)

    def copy(kind, slot, src, to):
        return pltpu.make_async_remote_copy(
            src_ref=buf.at[src],
            dst_ref=buf.at[src],
            send_sem=send.at[kind, slot],
            recv_sem=recv.at[src],
            device_id={"ctx": to},
            device_id_type=MESH,
        )

    def slow_peer(k):
        return (lax.rem(slow + k, slows) * 2 + mid) * 2 + last

    for k in range(1, slows):
        copy(0, k, me, slow_peer(k)).start()
    copy(1, me, me, mid_peer).start()
    copy(2, me, me, last_peer).start()
    use(me)

    @pl.loop(1, slows)
    def _(k):
        src = slow_peer(k)
        copy(0, k, src, mid_peer).wait_recv()
        copy(1, src, src, mid_peer).start()
        copy(2, src, src, last_peer).start()
        use(src)

    @pl.loop(0, slows)
    def _(k):
        src = (lax.rem(slow + k, slows) * 2 + (1 - mid)) * 2 + last
        copy(1, src, src, mid_peer).wait_recv()
        copy(2, src, src, last_peer).start()
        use(src)

    @pl.loop(0, slows * 2)
    def _(k):
        src = (lax.rem(slow + k // 2, slows) * 2 + lax.rem(mid + lax.rem(k, 2), 2)) * 2 + (1 - last)
        copy(2, src, src, last_peer).wait_recv()
        use(src)

    for k in range(1, slows):
        copy(0, k, me, slow_peer(k)).wait_send()

    @pl.loop(0, slows)
    def _(k):
        own = (k * 2 + mid) * 2 + last
        other = (k * 2 + (1 - mid)) * 2 + last
        copy(1, own, own, mid_peer).wait_send()
        copy(2, own, own, last_peer).wait_send()
        copy(2, other, other, last_peer).wait_send()


def kernel(n, E, top, q_ref, kv_ref, ids_ref, gate_ref, w_hbm, out_ref,
           q_all, meta_all, kv_all, g_all, dense, w_all, part_in, part_out, acc,
           kv_send, kv_recv, g_send, g_recv, q_send, q_recv, m_send, m_recv, p_send, p_recv, w_sem):
    ctx = lax.axis_index("ctx")
    me = lax.axis_index("exp")
    slows = n // 4
    slow, mid, last = ctx // 4, lax.rem(ctx // 2, 2), lax.rem(ctx, 2)
    coords = (slow, mid, last, slows)
    rows, hd = q_ref.shape
    tok_dev = rows // top
    span = kv_ref.shape[0]
    heads = kv_ref.shape[1] // (2 * hd)
    per_dev = EXPERTS // E
    group = per_dev // heads
    slots = g_all.shape[2] - META_ROWS
    cols = w_all.shape[1]
    keys = n * span

    w_copy = pltpu.make_async_copy(w_hbm, w_all, w_sem)
    w_copy.start()

    barrier = pltpu.get_barrier_semaphore()
    for k in range(1, slows):
        pl.semaphore_signal(barrier, inc=1, device_id={"ctx": (lax.rem(slow + k, slows) * 2 + mid) * 2 + last}, device_id_type=MESH)
    pl.semaphore_signal(barrier, inc=1, device_id={"ctx": (slow * 2 + 1 - mid) * 2 + last}, device_id_type=MESH)
    pl.semaphore_signal(barrier, inc=1, device_id={"ctx": (slow * 2 + mid) * 2 + 1 - last}, device_id_type=MESH)
    for k in range(1, E):
        pl.semaphore_signal(barrier, inc=1, device_id={"exp": lax.rem(me + k, E)}, device_id_type=MESH)

    diag = iota((rows, rows), 0) == iota((rows, rows), 1)

    def to_lanes(values):
        spread = jnp.concatenate(
            [jnp.broadcast_to(values[t : t + 1, :], (top, top)) for t in range(tok_dev)], 0
        )
        mine = lax.rem(iota((rows, top), 0), top) == iota((rows, top), 1)
        column = jnp.sum(jnp.where(mine, spread, 0.0), axis=1, keepdims=True)
        return jnp.sum(jnp.where(diag, column, 0.0), axis=0, keepdims=True)

    def to_column(lane_row):
        return jnp.sum(jnp.where(diag, lane_row, 0.0), axis=1, keepdims=True)

    gate_exp = jnp.exp(gate_ref[...])
    gates = (gate_exp / jnp.sum(gate_exp, axis=1, keepdims=True)).astype(BF16).astype(F32)
    meta_all[me] = jnp.concatenate(
        [
            jnp.broadcast_to(to_lanes(ids_ref[...].astype(F32)), (4, rows)),
            jnp.broadcast_to(to_lanes(gates), (4, rows)),
        ],
        0,
    )
    q_all[me] = q_ref[...]
    kv_all[ctx] = kv_ref[...]

    pl.semaphore_wait(barrier, slows - 1 + 2 + E - 1)

    def exchange(buf, send, recv, k, src):
        return pltpu.make_async_remote_copy(
            src_ref=buf.at[src],
            dst_ref=buf.at[src],
            send_sem=send.at[k],
            recv_sem=recv.at[src],
            device_id={"exp": lax.rem(me + k, E)},
            device_id_type=MESH,
        )

    for k in range(1, E):
        exchange(q_all, q_send, q_recv, k, me).start()
        exchange(meta_all, m_send, m_recv, k, me).start()
    flood(kv_all, kv_send, kv_recv, coords, n, lambda src: None)
    for k in range(1, E):
        src = lax.rem(me + k, E)
        exchange(q_all, q_send, q_recv, k, src).wait_recv()
        exchange(meta_all, m_send, m_recv, k, src).wait_recv()

    @pl.loop(0, E)
    def _(b):
        meta = meta_all[b]
        local = meta[0:1, :] - (me * per_dev).astype(F32)
        inside_row = (local >= 0.0) & (local < per_dev)
        local_col = to_column(local)
        gate_col = to_column(meta[4:5, :])
        inside_col = (local_col >= 0.0) & (local_col < per_dev)
        q = q_all[b]
        scores = jnp.zeros((rows, keys), F32)
        of_head = [
            (local_col >= h * group) & (local_col < (h + 1) * group) for h in range(heads)
        ]
        for h in range(heads):
            k_h = kv_all[:, :, h * hd : (h + 1) * hd].reshape(keys, hd)
            s_h = lax.dot_general(q, k_h, (((1,), (1,)), ((), ())), preferred_element_type=F32)
            scores = jnp.where(of_head[h], s_h, scores)
        scores = scores * hd ** (-0.5)
        first = (b * n + ctx) * tok_dev
        visible = iota((rows, keys), 1) <= first + iota((rows, keys), 0) // top
        scores = jnp.where(visible, scores, -1e30)
        peak = jnp.max(scores, axis=1, keepdims=True)
        weights = jnp.where(visible, jnp.exp(scores - peak), 0.0)
        total = jnp.sum(weights, axis=1, keepdims=True)
        mixed = jnp.zeros((rows, hd), F32)
        for h in range(heads):
            v_h = kv_all[:, :, (heads + h) * hd : (heads + h + 1) * hd].reshape(keys, hd)
            mixed += jnp.dot(
                jnp.where(of_head[h], weights, 0.0).astype(BF16), v_h, preferred_element_type=F32
            )
        gated = (gate_col * (mixed / total)).astype(BF16)
        before = (iota((rows, rows), 0) < iota((rows, rows), 1)) & inside_col
        rank_row = jnp.sum(jnp.where(before, 1.0, 0.0), axis=0, keepdims=True)
        slot_row = jnp.where(inside_row, rank_row, -1.0)
        slot_col = to_column(slot_row)
        pick = (iota((slots, rows), 0).astype(F32) == slot_row).astype(F32).astype(BF16)
        packed = jnp.dot(pick, gated, preferred_element_type=F32).astype(BF16)
        place = local_col * tok_dev + (iota((rows, 1), 0) // top).astype(F32)
        placed = slot_col == iota((rows, LANES), 1).astype(F32)
        target = jnp.sum(jnp.where(placed, place + 1.0, 0.0), axis=0, keepdims=True) - 1.0
        g_all[ctx, b, 0:slots, :] = packed
        g_all[ctx, b, slots : slots + META_ROWS, :] = jnp.broadcast_to(
            target, (META_ROWS, LANES)
        ).astype(BF16)

    def expand(src):
        for b in range(E):
            shard = g_all[src, b]
            target = shard[slots:, :].astype(F32)[0:1, : slots + META_ROWS]
            where = (
                iota((per_dev * tok_dev, slots + META_ROWS), 0).astype(F32) == target
            ).astype(F32).astype(BF16)
            spread = jnp.dot(where, shard, preferred_element_type=F32)
            at = pl.ds(pl.multiple_of((b * n + src) * tok_dev, tok_dev), tok_dev)
            for x in range(per_dev):
                dense[at, x * hd : (x + 1) * hd] = spread[x * tok_dev : (x + 1) * tok_dev, :]

    flood(g_all, g_send, g_recv, coords, n, expand)
    w_copy.wait()

    half = n * tok_dev
    depth = per_dev * hd
    chunk = min(512, depth)

    def project(b):
        acc[...] = jnp.zeros_like(acc)
        base = pl.multiple_of(b * half, half)

        @pl.loop(0, depth // chunk)
        def _(j):
            at = pl.ds(pl.multiple_of(j * chunk, chunk), chunk)
            acc[...] += jnp.dot(
                dense[pl.ds(base, half), at].astype(BF16), w_all[at, :], preferred_element_type=F32
            )

    def send_part(k):
        return pltpu.make_async_remote_copy(
            src_ref=part_out.at[k],
            dst_ref=part_in.at[E - k],
            send_sem=p_send.at[k],
            recv_sem=p_recv.at[E - k],
            device_id={"exp": lax.rem(me + k, E)},
            device_id_type=MESH,
        )

    for k in range(1, E):
        project(lax.rem(me + k, E))
        part_out[k] = acc[...].astype(BF16)
        send_part(k).start()
    project(me)
    total = acc[...].astype(BF16).astype(F32)
    for k in range(1, E):
        send_part(E - k).wait_recv()
        total += part_in[k].astype(F32)
    out_ref[...] = total.astype(BF16)
    for k in range(1, E):
        send_part(k).wait_send()
        exchange(q_all, q_send, q_recv, k, me).wait_send()
        exchange(meta_all, m_send, m_recv, k, me).wait_send()


def body(queries, key_heads, value_heads, expert_ids, gate_logits, out_weight):
    n = lax.axis_size("ctx")
    E = lax.axis_size("exp")
    tok_dev, top, hd = queries.shape
    rows = tok_dev * top
    span, heads, _ = key_heads.shape
    per_dev, _, cols = out_weight.shape
    slots = -(-per_dev * MOST // 16) * 16
    kv = jnp.concatenate(
        [key_heads.reshape(span, heads * hd), value_heads.reshape(span, heads * hd)], axis=1
    )
    vmem = pl.BlockSpec(memory_space=pltpu.VMEM)
    dma = pltpu.SemaphoreType.DMA
    return pl.pallas_call(
        functools.partial(kernel, n, E, top),
        out_shape=jax.ShapeDtypeStruct((n * tok_dev, cols), BF16),
        in_specs=[vmem] * 4 + [pl.BlockSpec(memory_space=pl.ANY)],
        out_specs=vmem,
        scratch_shapes=[
            pltpu.VMEM((E, rows, hd), BF16),
            pltpu.VMEM((E, 8, rows), F32),
            pltpu.VMEM((n, span, 2 * heads * hd), BF16),
            pltpu.VMEM((n, E, slots + META_ROWS, hd), BF16),
            pltpu.VMEM((E * n * tok_dev, per_dev * hd), F32),
            pltpu.VMEM((per_dev * hd, cols), BF16),
            pltpu.VMEM((E, n * tok_dev, cols), BF16),
            pltpu.VMEM((E, n * tok_dev, cols), BF16),
            pltpu.VMEM((n * tok_dev, cols), F32),
            dma((3, n)), dma((n,)), dma((3, n)), dma((n,)),
            dma((E,)), dma((E,)), dma((E,)), dma((E,)), dma((E,)), dma((E,)),
            dma,
        ],
        compiler_params=pltpu.CompilerParams(
            collective_id=0, has_side_effects=True, vmem_limit_bytes=50 * 2**20
        ),
    )(queries.reshape(rows, hd), kv, expert_ids, gate_logits, out_weight.reshape(per_dev * hd, cols))


def solution(mesh):
    in_specs = (
        P(("exp", "ctx"), None, None),
        P("ctx", "exp", None),
        P("ctx", "exp", None),
        P(("exp", "ctx"), None),
        P(("exp", "ctx"), None),
        P("exp", None, "ctx"),
    )
    out_specs = P("exp", "ctx")
    return jax.shard_map(body, mesh=mesh, in_specs=in_specs, out_specs=out_specs, check_vma=False)
```

time: 171 us -> 39.3 us (0.23)
  blocking collectives: 80 us -> 0 us
  Pallas kernels: 0 us -> 35.4 us
  other arithmetic: 22.7 us -> 0.01 us
  local copies, waits for them, and re-layouts: 23.5 us -> 3.52 us
  waiting for transfers between devices: 14.6 us -> 0 us
  between operations: 13.5 us -> 0.02 us
  starting transfers between devices: 10.8 us -> 0 us
  matrix products: 4.73 us -> 0 us
    all_gather x4 -> x0, blocking collectives: 80 us -> none  [the longest x2 39.1 us: body(): lax.all_gather((gated_grid, pos_grid), 'ctx', axis=0, tiled=True)]
    pallas_call x0 -> x1, Pallas kernels: none -> 35.4 us  [body(): pl.pallas_call(functools.partial(kernel, n, E, top), out_shape=jax.ShapeD...]
    scatter-add x1 -> x0, other arithmetic: 19.3 us -> none  [body(): jax.ops.segment_sum(projected.reshape(-1, projected.shape[-1]), segment.r...]
    reshape x4 -> x1, local copies, waits for them, and re-layouts: 12.2 us -> 0.74 us  [body(): value_heads.reshape(span, heads * hd)]
    reduce_scatter x1 -> x0, waiting for transfers between devices: 10.9 us -> none  [body(): lax.psum_scatter(partial_term.astype(jnp.bfloat16), 'exp', scatter_dimens...]
    all_to_all x3 -> x0, starting transfers between devices: 10.7 us -> none  [the longest x1 4.21 us: body(): lax.all_to_all(send_gate.reshape(layout), 'exp', split_axis=0, concat_axi...]
    transpose x1 -> x0, local copies, waits for them, and re-layouts: 7.54 us -> none  [body(): jnp.einsum('chsgmd,hgdo->chsgmo', gated_piece, weight_grid, preferred_ele...]
    dot_general x4 -> x0, matrix products: 4.73 us -> none  [the longest x1 3.43 us: body(): jnp.einsum('chsgmd,hgdo->chsgmo', gated_piece, weight_grid, preferred_ele...]
  transfers between devices with their start and end apart: 4 -> 0, of which waited for: 2 -> 0; matrix products, arithmetic and copies ran while one was open for 3% -> 0% of each run, Pallas kernels for 0% -> 0%
where the time goes in v1:
time: 39.3 us; the launch traced here: 38.9 us
  Pallas kernels  35.4 us (90%)
  local copies, waits for them, and re-layouts  3.52 us (9%)
    pallas_call x1, Pallas kernels, body(): pl.pallas_call(functools.partial(kernel, n, E, top), out_shape=jax.ShapeD...  35.4 us
    unnamed x7, local copies, waits for them, and re-layouts  2.78 us

profile of v1, /device:TPU:0, one launch (start us, length us, event | category | flops | bytes accessed | tf_op | source)
XLA Modules:
  0.0 38.9 jit_solution(6608659072724623104)
XLA Ops:
  0.0 0.7 %copy_bitcast_fusion = (bf16[16,512]{1,0:T(8,128)(2,1)S(1)}, bf16[16,512]{1,0:T(8,128)(2,1)S(1)}) fusion(bf16[2,8,4,128]{3,2,1,0:T(4,128)(2,1)} %bitcast.10, bf16[2,8,4,128]{3,2,1,0:T(4,128)(2,1)} %bitcast.11), kind=kLoop, calls=%fused_computation.1 | loop fusion | bytes 65536 | tf_op jit(solution)/shard_map/reshape | solution.py:266
  0.7 0.0 copy-start
  0.8 0.7 %copy-done = bf16[8,16,128]{2,1,0:T(8,128)(2,1)S(1)} copy-done((bf16[8,16,128]{2,1,0:T(8,128)(2,1)S(1)}, bf16[8,16,128]{2,1,0:T(8,128)(2,1)}, u32[]{:S(2)}) %copy-start) | copy-done | bytes 32792
  1.5 0.0 copy-start.1
  1.5 0.7 %copy-done.1 = s32[8,16]{1,0:T(8,128)S(1)} copy-done((s32[8,16]{1,0:T(8,128)S(1)}, s32[8,16]{1,0:T(8,128)}, u32[]{:S(2)}) %copy-start.1) | copy-done | bytes 536
  2.2 0.0 copy-start.2
  2.2 0.7 %copy-done.2 = f32[8,16]{1,0:T(8,128)S(1)} copy-done((f32[8,16]{1,0:T(8,128)S(1)}, f32[8,16]{1,0:T(8,128)}, u32[]{:S(2)}) %copy-start.2) | copy-done | bytes 536
  2.9 35.4 %shard_map.64 = bf16[128,512]{1,0:T(8,128)(2,1)S(1)} custom-call(bf16[128,128]{1,0:T(8,128)(2,1)S(1)} %bitcast.8, bf16[16,1024]{1,0:T(8,128)(2,1)S(1)} %pad_maximum_fusion.kv_ref, s32[8,16]{1,0:T(8,128)S(1)} %copy-done.1, f32[8,16]{1,0:T(8,128)S(1)} %copy-done.2, bf16[4096,512]{1,0:T(8,128)(2,1)} %bitcast.9), custom_call_target="tpu_custom_call" | custom-call | tf_op jit(solution)/shard_map/pallas_call | solution.py:270
  38.3 0.7 %copy.12 = bf16[128,512]{1,0:T(8,128)(2,1)} copy(bf16[128,512]{1,0:T(8,128)(2,1)S(1)} %shard_map.64) | data formatting | bytes 262144
  (1 shorter events, 0.0 us)
Async XLA Ops:
  0.7 0.8 %copy-start = (bf16[8,16,128]{2,1,0:T(8,128)(2,1)S(1)}, bf16[8,16,128]{2,1,0:T(8,128)(2,1)}, u32[]{:S(2)}) copy-start(bf16[8,16,128]{2,1,0:T(8,128)(2,1)} %param.6) | copy-start | bytes 98308
  1.5 0.7 %copy-start.1 = (s32[8,16]{1,0:T(8,128)S(1)}, s32[8,16]{1,0:T(8,128)}, u32[]{:S(2)}) copy-start(s32[8,16]{1,0:T(8,128)} %ids_ref.1) | copy-start | bytes 1540
  2.2 0.7 %copy-start.2 = (f32[8,16]{1,0:T(8,128)S(1)}, f32[8,16]{1,0:T(8,128)}, u32[]{:S(2)}) copy-start(f32[8,16]{1,0:T(8,128)} %gate_ref.1) | copy-start | bytes 1540

commit v2 on v1

v2 whole, which is shorter than its diff:
```python
import functools

import jax
import jax.numpy as jnp
from jax import lax
from jax.experimental import pallas as pl
from jax.experimental.pallas import tpu as pltpu
from jax.sharding import PartitionSpec as P

EXPERTS = 64
MOST = 3
LANES = 128
META_ROWS = 16
F32 = jnp.float32
BF16 = jnp.bfloat16
MESH = pl.DeviceIdType.MESH


def iota(shape, dim):
    return lax.broadcasted_iota(jnp.int32, shape, dim)


class Flood:
    def __init__(self, buf, send, recv, ctx, n):
        self.buf, self.send, self.recv = buf, send, recv
        self.units, self.slows, self.me = buf.shape[1], n // 4, ctx
        self.slow, self.mid, self.last = ctx // 4, lax.rem(ctx // 2, 2), lax.rem(ctx, 2)
        self.mid_peer = (self.slow * 2 + (1 - self.mid)) * 2 + self.last
        self.last_peer = (self.slow * 2 + self.mid) * 2 + (1 - self.last)

    def copy(self, kind, slot, src, u, to):
        return pltpu.make_async_remote_copy(
            src_ref=self.buf.at[src, u],
            dst_ref=self.buf.at[src, u],
            send_sem=self.send.at[kind, slot, u],
            recv_sem=self.recv.at[src, u],
            device_id={"ctx": to},
            device_id_type=MESH,
        )

    def slow_peer(self, k):
        return (lax.rem(self.slow + k, self.slows) * 2 + self.mid) * 2 + self.last

    def over_mid(self, src, u):
        return self.copy(1, src, src, u, self.mid_peer)

    def over_last(self, src, u):
        return self.copy(2, src, src, u, self.last_peer)

    def begin(self, u):
        for k in range(1, self.slows):
            self.copy(0, k, self.me, u, self.slow_peer(k)).start()
        self.over_mid(self.me, u).start()
        self.over_last(self.me, u).start()

    def from_slow(self, u, use):
        @pl.loop(1, self.slows)
        def _(k):
            src = self.slow_peer(k)
            self.over_mid(src, u).wait_recv()
            self.over_mid(src, u).start()
            self.over_last(src, u).start()
            use(src, u)

    def from_mid(self, u, use):
        @pl.loop(0, self.slows)
        def _(k):
            src = (lax.rem(self.slow + k, self.slows) * 2 + (1 - self.mid)) * 2 + self.last
            self.over_mid(src, u).wait_recv()
            self.over_last(src, u).start()
            use(src, u)

    def from_last(self, u, use):
        @pl.loop(0, self.slows * 2)
        def _(k):
            m = lax.rem(self.mid + k // self.slows, 2)
            src = (lax.rem(self.slow + k, self.slows) * 2 + m) * 2 + (1 - self.last)
            self.over_last(src, u).wait_recv()
            use(src, u)

    def end(self):
        @pl.loop(0, self.units)
        def _(u):
            for k in range(1, self.slows):
                self.copy(0, k, self.me, u, self.slow_peer(k)).wait_send()

            @pl.loop(0, self.slows)
            def _(k):
                own = (k * 2 + self.mid) * 2 + self.last
                other = (k * 2 + (1 - self.mid)) * 2 + self.last
                self.over_mid(own, u).wait_send()
                self.over_last(own, u).wait_send()
                self.over_last(other, u).wait_send()


def kernel(n, E, top, q_hbm, k_hbm, v_hbm, ids_hbm, gate_hbm, w_hbm, out_ref,
           k_ref, v_ref, ids_ref, gate_ref, q_all, meta_all, kv_all, g_all, dense, w_all, part_in, part_out, acc,
           kv_send, kv_recv, g_send, g_recv, q_send, q_recv, m_send, m_recv, p_send, p_recv, w_sem, in_sem):
    ctx = lax.axis_index("ctx")
    me = lax.axis_index("exp")
    slows = n // 4
    slow, mid, last = ctx // 4, lax.rem(ctx // 2, 2), lax.rem(ctx, 2)
    rows, hd = q_hbm.shape
    tok_dev = rows // top
    span, heads = k_hbm.shape[0], k_hbm.shape[1]
    per_dev = EXPERTS // E
    group = per_dev // heads
    slots = g_all.shape[2] - META_ROWS
    keys = n * span

    inputs = [
        pltpu.make_async_copy(a, b, in_sem.at[k])
        for k, (a, b) in enumerate(
            [(k_hbm, k_ref), (v_hbm, v_ref), (ids_hbm, ids_ref), (gate_hbm, gate_ref), (q_hbm, q_all.at[me])]
        )
    ]
    for copy in inputs:
        copy.start()
    w_copy = pltpu.make_async_copy(w_hbm, w_all, w_sem)

    barrier = pltpu.get_barrier_semaphore()
    for k in range(1, slows):
        pl.semaphore_signal(barrier, inc=1, device_id={"ctx": (lax.rem(slow + k, slows) * 2 + mid) * 2 + last}, device_id_type=MESH)
    pl.semaphore_signal(barrier, inc=1, device_id={"ctx": (slow * 2 + 1 - mid) * 2 + last}, device_id_type=MESH)
    pl.semaphore_signal(barrier, inc=1, device_id={"ctx": (slow * 2 + mid) * 2 + 1 - last}, device_id_type=MESH)
    for k in range(1, E):
        pl.semaphore_signal(barrier, inc=1, device_id={"exp": lax.rem(me + k, E)}, device_id_type=MESH)

    for copy in inputs:
        copy.wait()
    diag = iota((rows, rows), 0) == iota((rows, rows), 1)

    def to_lanes(values):
        spread = jnp.concatenate(
            [jnp.broadcast_to(values[t : t + 1, :], (top, top)) for t in range(tok_dev)], 0
        )
        mine = lax.rem(iota((rows, top), 0), top) == iota((rows, top), 1)
        column = jnp.sum(jnp.where(mine, spread, 0.0), axis=1, keepdims=True)
        return jnp.sum(jnp.where(diag, column, 0.0), axis=0, keepdims=True)

    def to_column(lane_row):
        return jnp.sum(jnp.where(diag, lane_row, 0.0), axis=1, keepdims=True)

    gate_exp = jnp.exp(gate_ref[...])
    gates = (gate_exp / jnp.sum(gate_exp, axis=1, keepdims=True)).astype(BF16).astype(F32)
    meta_all[me] = jnp.concatenate(
        [
            jnp.broadcast_to(to_lanes(ids_ref[...].astype(F32)), (4, rows)),
            jnp.broadcast_to(to_lanes(gates), (4, rows)),
        ],
        0,
    )
    for h in range(heads):
        kv_all[ctx, 0, :, h * hd : (h + 1) * hd] = k_ref[...].astype(F32)[:, h, :].astype(BF16)
        kv_all[ctx, 0, :, (heads + h) * hd : (heads + h + 1) * hd] = v_ref[...].astype(F32)[:, h, :].astype(BF16)

    pl.semaphore_wait(barrier, slows - 1 + 2 + E - 1)

    def exchange(buf, send, recv, k, src):
        return pltpu.make_async_remote_copy(
            src_ref=buf.at[src],
            dst_ref=buf.at[src],
            send_sem=send.at[k],
            recv_sem=recv.at[src],
            device_id={"exp": lax.rem(me + k, E)},
            device_id_type=MESH,
        )

    kv_flood = Flood(kv_all, kv_send, kv_recv, ctx, n)
    g_flood = Flood(g_all, g_send, g_recv, ctx, n)
    kv_flood.begin(0)
    for k in range(1, E):
        exchange(q_all, q_send, q_recv, k, me).start()
        exchange(meta_all, m_send, m_recv, k, me).start()
    w_copy.start()
    for step in (kv_flood.from_slow, kv_flood.from_mid, kv_flood.from_last):
        step(0, lambda src, u: None)
    for k in range(1, E):
        src = lax.rem(me + k, E)
        exchange(q_all, q_send, q_recv, k, src).wait_recv()
        exchange(meta_all, m_send, m_recv, k, src).wait_recv()

    @pl.loop(0, E)
    def _(i):
        b = lax.rem(me + 1 + i, E)
        meta = meta_all[b]
        local = meta[0:1, :] - (me * per_dev).astype(F32)
        inside_row = (local >= 0.0) & (local < per_dev)
        local_col = to_column(local)
        gate_col = to_column(meta[4:5, :])
        inside_col = (local_col >= 0.0) & (local_col < per_dev)
        q = q_all[b]
        scores = jnp.zeros((rows, keys), F32)
        of_head = [
            (local_col >= h * group) & (local_col < (h + 1) * group) for h in range(heads)
        ]
        for h in range(heads):
            k_h = kv_all[:, 0, :, h * hd : (h + 1) * hd].reshape(keys, hd)
            s_h = lax.dot_general(q, k_h, (((1,), (1,)), ((), ())), preferred_element_type=F32)
            scores = jnp.where(of_head[h], s_h, scores)
        scores = scores * hd ** (-0.5)
        first = (b * n + ctx) * tok_dev
        visible = iota((rows, keys), 1) <= first + iota((rows, keys), 0) // top
        scores = jnp.where(visible, scores, -1e30)
        peak = jnp.max(scores, axis=1, keepdims=True)
        weights = jnp.where(visible, jnp.exp(scores - peak), 0.0)
        total = jnp.sum(weights, axis=1, keepdims=True)
        mixed = jnp.zeros((rows, hd), F32)
        for h in range(heads):
            v_h = kv_all[:, 0, :, (heads + h) * hd : (heads + h + 1) * hd].reshape(keys, hd)
            mixed += jnp.dot(
                jnp.where(of_head[h], weights, 0.0).astype(BF16), v_h, preferred_element_type=F32
            )
        gated = (gate_col * (mixed / total)).astype(BF16)
        before = (iota((rows, rows), 0) < iota((rows, rows), 1)) & inside_col
        rank_row = jnp.sum(jnp.where(before, 1.0, 0.0), axis=0, keepdims=True)
        slot_row = jnp.where(inside_row, rank_row, -1.0)
        slot_col = to_column(slot_row)
        pick = (iota((slots, rows), 0).astype(F32) == slot_row).astype(F32).astype(BF16)
        packed = jnp.dot(pick, gated, preferred_element_type=F32).astype(BF16)
        place = local_col * tok_dev + (iota((rows, 1), 0) // top).astype(F32)
        placed = slot_col == iota((rows, LANES), 1).astype(F32)
        target = jnp.sum(jnp.where(placed, place + 1.0, 0.0), axis=0, keepdims=True) - 1.0
        g_all[ctx, b, 0:slots, :] = packed
        g_all[ctx, b, slots : slots + META_ROWS, :] = jnp.broadcast_to(
            target, (META_ROWS, LANES)
        ).astype(BF16)
        g_flood.begin(b)

    def expand(src, b):
        shard = g_all[src, b]
        target = shard[slots:, :].astype(F32)[0:1, : slots + META_ROWS]
        where = (
            iota((per_dev * tok_dev, slots + META_ROWS), 0).astype(F32) == target
        ).astype(F32).astype(BF16)
        spread = jnp.dot(where, shard, preferred_element_type=F32)
        at = pl.ds(pl.multiple_of((b * n + src) * tok_dev, tok_dev), tok_dev)
        for x in range(per_dev):
            dense[at, x * hd : (x + 1) * hd] = spread[x * tok_dev : (x + 1) * tok_dev, :]

    half = n * tok_dev
    depth = per_dev * hd
    chunk = min(512, depth)
    parts, width = part_in.shape[1], part_in.shape[3]

    def project(b, p):
        acc[...] = jnp.zeros_like(acc)
        base = pl.multiple_of(b * half, half)

        @pl.loop(0, depth // chunk)
        def _(j):
            at = pl.ds(pl.multiple_of(j * chunk, chunk), chunk)
            acc[...] += jnp.dot(
                dense[pl.ds(base, half), at].astype(BF16),
                w_all[at, p * width : (p + 1) * width],
                preferred_element_type=F32,
            )
        return acc[...].astype(BF16)

    def send_part(k, p):
        return pltpu.make_async_remote_copy(
            src_ref=part_out.at[k, p],
            dst_ref=part_in.at[E - k, p],
            send_sem=p_send.at[k, p],
            recv_sem=p_recv.at[E - k, p],
            device_id={"exp": lax.rem(me + k, E)},
            device_id_type=MESH,
        )

    w_copy.wait()
    halves = [lax.rem(me + 1 + i, E) for i in range(E)]

    def finish(i):
        k = (i + 1) % E
        for p in range(parts):
            part_out[k, p] = project(halves[i], p)
            if k:
                send_part(k, p).start()

    for i in range(E):
        g_flood.from_slow(halves[i], expand)
        if i:
            g_flood.from_last(halves[i - 1], expand)
            expand(ctx, halves[i - 1])
            finish(i - 1)
        g_flood.from_mid(halves[i], expand)
    g_flood.from_last(me, expand)
    expand(ctx, me)
    finish(E - 1)
    kv_flood.end()
    g_flood.end()
    for k in range(1, E):
        exchange(q_all, q_send, q_recv, k, me).wait_send()
        exchange(meta_all, m_send, m_recv, k, me).wait_send()
    for p in range(parts):
        total = part_out[0, p].astype(F32)
        for k in range(1, E):
            send_part(E - k, p).wait_recv()
            total += part_in[k, p].astype(F32)
        out_ref[:, p * width : (p + 1) * width] = total.astype(BF16)
    for k in range(1, E):
        for p in range(parts):
            send_part(k, p).wait_send()


def body(queries, key_heads, value_heads, expert_ids, gate_logits, out_weight):
    n = lax.axis_size("ctx")
    E = lax.axis_size("exp")
    tok_dev, top, hd = queries.shape
    rows = tok_dev * top
    span, heads, _ = key_heads.shape
    per_dev, _, cols = out_weight.shape
    slots = -(-per_dev * MOST // 16) * 16
    parts = max(1, cols // 256)
    vmem = pl.BlockSpec(memory_space=pltpu.VMEM)
    dma = pltpu.SemaphoreType.DMA
    return pl.pallas_call(
        functools.partial(kernel, n, E, top),
        out_shape=jax.ShapeDtypeStruct((n * tok_dev, cols), BF16),
        in_specs=[pl.BlockSpec(memory_space=pltpu.HBM)] * 6,
        out_specs=vmem,
        scratch_shapes=[
            pltpu.VMEM((span, heads, hd), BF16),
            pltpu.VMEM((span, heads, hd), BF16),
            pltpu.VMEM((tok_dev, top), jnp.int32),
            pltpu.VMEM((tok_dev, top), F32),
            pltpu.VMEM((E, rows, hd), BF16),
            pltpu.VMEM((E, 8, rows), F32),
            pltpu.VMEM((n, 1, span, 2 * heads * hd), BF16),
            pltpu.VMEM((n, E, slots + META_ROWS, hd), BF16),
            pltpu.VMEM((E * n * tok_dev, per_dev * hd), F32),
            pltpu.VMEM((per_dev * hd, cols), BF16),
            pltpu.VMEM((E, parts, n * tok_dev, cols // parts), BF16),
            pltpu.VMEM((E, parts, n * tok_dev, cols // parts), BF16),
            pltpu.VMEM((n * tok_dev, cols // parts), F32),
            dma((3, n, 1)), dma((n, 1)), dma((3, n, E)), dma((n, E)),
            dma((E,)), dma((E,)), dma((E,)), dma((E,)), dma((E, parts)), dma((E, parts)),
            dma, dma((5,)),
        ],
        compiler_params=pltpu.CompilerParams(
            collective_id=0, has_side_effects=True, vmem_limit_bytes=50 * 2**20
        ),
    )(queries.reshape(rows, hd), key_heads, value_heads, expert_ids, gate_logits, out_weight.reshape(per_dev * hd, cols))


def solution(mesh):
    in_specs = (
        P(("exp", "ctx"), None, None),
        P("ctx", "exp", None),
        P("ctx", "exp", None),
        P(("exp", "ctx"), None),
        P(("exp", "ctx"), None),
        P("exp", None, "ctx"),
    )
    out_specs = P("exp", "ctx")
    return jax.shard_map(body, mesh=mesh, in_specs=in_specs, out_specs=out_specs, check_vma=False)
```

time: 39.3 us -> 37.6 us (0.957)
  Pallas kernels: 35.4 us -> 33 us
  local copies, waits for them, and re-layouts: 3.52 us -> 4.22 us
    pallas_call x1, Pallas kernels: 35.4 us -> 33 us  [body(): pl.pallas_call(functools.partial(kernel, n, E, top), out_shape=jax.ShapeD...]
    unnamed x7 -> x11, local copies, waits for them, and re-layouts: 2.78 us -> 4.22 us
    reshape x1 -> x0, local copies, waits for them, and re-layouts: 0.74 us -> none  [body(): value_heads.reshape(span, heads * hd)]
where the time goes in v2:
time: 37.6 us; the launch traced here: 37.2 us
  Pallas kernels  33 us (88%)
  local copies, waits for them, and re-layouts  4.22 us (11%)
    pallas_call x1, Pallas kernels, body(): pl.pallas_call(functools.partial(kernel, n, E, top), out_shape=jax.ShapeD...  33 us
    unnamed x11, local copies, waits for them, and re-layouts  4.22 us

profile of v2, /device:TPU:0, one launch (start us, length us, event | category | flops | bytes accessed | tf_op | source)
XLA Modules:
  0.0 37.2 jit_solution(1197512047571520163)
XLA Ops:
  0.0 0.0 copy-start
  0.0 0.8 %copy-done = bf16[8,16,128]{2,1,0:T(8,128)(2,1)S(1)} copy-done((bf16[8,16,128]{2,1,0:T(8,128)(2,1)S(1)}, bf16[8,16,128]{2,1,0:T(8,128)(2,1)}, u32[]{:S(2)}) %copy-start) | copy-done | bytes 32792
  0.8 0.0 copy-start.1
  0.8 0.7 %copy-done.1 = bf16[16,4,128]{2,1,0:T(4,128)(2,1)S(1)} copy-done((bf16[16,4,128]{2,1,0:T(4,128)(2,1)S(1)}, bf16[16,4,128]{2,1,0:T(4,128)(2,1)}, u32[]{:S(2)}) %copy-start.1) | copy-done | bytes 16408
  1.5 0.0 copy-start.2
  1.5 0.7 %copy-done.2 = bf16[16,4,128]{2,1,0:T(4,128)(2,1)S(1)} copy-done((bf16[16,4,128]{2,1,0:T(4,128)(2,1)S(1)}, bf16[16,4,128]{2,1,0:T(4,128)(2,1)}, u32[]{:S(2)}) %copy-start.2) | copy-done | bytes 16408
  2.2 0.0 copy-start.3
  2.2 0.7 %copy-done.3 = s32[8,16]{1,0:T(8,128)S(1)} copy-done((s32[8,16]{1,0:T(8,128)S(1)}, s32[8,16]{1,0:T(8,128)}, u32[]{:S(2)}) %copy-start.3) | copy-done | bytes 536
  2.9 0.0 copy-start.4
  2.9 0.7 %copy-done.4 = f32[8,16]{1,0:T(8,128)S(1)} copy-done((f32[8,16]{1,0:T(8,128)S(1)}, f32[8,16]{1,0:T(8,128)}, u32[]{:S(2)}) %copy-start.4) | copy-done | bytes 536
  3.6 33.0 %shard_map.64 = bf16[128,512]{1,0:T(8,128)(2,1)S(1)} custom-call(bf16[128,128]{1,0:T(8,128)(2,1)S(1)} %bitcast.2, bf16[16,4,128]{2,1,0:T(4,128)(2,1)S(1)} %copy-done.1, bf16[16,4,128]{2,1,0:T(4,128)(2,1)S(1)} %copy-done.2, s32[8,16]{1,0:T(8,128)S(1)} %copy-done.3, f32[8,16]{1,0:T(8,128)S(1)} %copy-done.4, bf16[4096,512]{1,0:T(8,128)(2,1)} %bitcast.3), custom_call_target="tpu_custom_call" | custom-call | tf_op jit(solution)/shard_map/pallas_call | solution.py:317
  36.5 0.7 %copy.8 = bf16[128,512]{1,0:T(8,128)(2,1)} copy(bf16[128,512]{1,0:T(8,128)(2,1)S(1)} %shard_map.64) | data formatting | bytes 262144
Async XLA Ops:
  0.0 0.8 %copy-start = (bf16[8,16,128]{2,1,0:T(8,128)(2,1)S(1)}, bf16[8,16,128]{2,1,0:T(8,128)(2,1)}, u32[]{:S(2)}) copy-start(bf16[8,16,128]{2,1,0:T(8,128)(2,1)} %param.6) | copy-start | bytes 98308
  0.8 0.7 %copy-start.1 = (bf16[16,4,128]{2,1,0:T(4,128)(2,1)S(1)}, bf16[16,4,128]{2,1,0:T(4,128)(2,1)}, u32[]{:S(2)}) copy-start(bf16[16,4,128]{2,1,0:T(4,128)(2,1)} %k_hbm.1) | copy-start | bytes 49156
  1.5 0.7 %copy-start.2 = (bf16[16,4,128]{2,1,0:T(4,128)(2,1)S(1)}, bf16[16,4,128]{2,1,0:T(4,128)(2,1)}, u32[]{:S(2)}) copy-start(bf16[16,4,128]{2,1,0:T(4,128)(2,1)} %v_hbm.1) | copy-start | bytes 49156
  2.2 0.7 %copy-start.3 = (s32[8,16]{1,0:T(8,128)S(1)}, s32[8,16]{1,0:T(8,128)}, u32[]{:S(2)}) copy-start(s32[8,16]{1,0:T(8,128)} %ids_hbm.1) | copy-start | bytes 1540
  2.9 0.7 %copy-start.4 = (f32[8,16]{1,0:T(8,128)S(1)}, f32[8,16]{1,0:T(8,128)}, u32[]{:S(2)}) copy-start(f32[8,16]{1,0:T(8,128)} %gate_hbm.1) | copy-start | bytes 1540

commit v3 on v2

--- a/solution.py
+++ b/solution.py
@@ -338,7 +338,7 @@
             dma, dma((5,)),
         ],
         compiler_params=pltpu.CompilerParams(
-            collective_id=0, has_side_effects=True, vmem_limit_bytes=50 * 2**20
+            collective_id=0, has_side_effects=True, vmem_limit_bytes=54 * 2**20
         ),
     )(queries.reshape(rows, hd), key_heads, value_heads, expert_ids, gate_logits, out_weight.reshape(per_dev * hd, cols))
 

time: 37.6 us -> 35.3 us (0.939)
  local copies, waits for them, and re-layouts: 4.22 us -> 1.57 us
  Pallas kernels: 33 us -> 33.5 us
    unnamed x11 -> x1, local copies, waits for them, and re-layouts: 4.22 us -> 1.57 us
    pallas_call x1, Pallas kernels: 33 us -> 33.5 us  [body(): pl.pallas_call(functools.partial(kernel, n, E, top), out_shape=jax.ShapeD...]
where the time goes in v3:
time: 35.3 us; the launch traced here: 35.1 us
  Pallas kernels  33.5 us (95%)
  local copies, waits for them, and re-layouts  1.57 us (4%)
    pallas_call x1, Pallas kernels, body(): pl.pallas_call(functools.partial(kernel, n, E, top), out_shape=jax.ShapeD...  33.5 us
    unnamed x1, local copies, waits for them, and re-layouts  1.57 us

profile of v3, /device:TPU:0, one launch (start us, length us, event | category | flops | bytes accessed | tf_op | source)
XLA Modules:
  0.0 35.1 jit_solution(3178231892592833276)
XLA Ops:
  0.0 33.5 %shard_map.64 = bf16[128,512]{1,0:T(8,128)(2,1)} custom-call(bf16[128,128]{1,0:T(8,128)(2,1)} %bitcast.3, bf16[16,4,128]{2,1,0:T(4,128)(2,1)} %k_hbm.1, bf16[16,4,128]{2,1,0:T(4,128)(2,1)} %v_hbm.1, s32[8,16]{1,0:T(8,128)} %ids_hbm.1, f32[8,16]{1,0:T(8,128)} %gate_hbm.1, bf16[4096,512]{1,0:T(8,128)(2,1)} %bitcast.2), custom_call_target="tpu_custom_call" | custom-call | tf_op jit(solution)/shard_map/pallas_call | solution.py:317
  33.5 1.6 %copy.8 = bf16[128,512]{1,0:T(8,128)(2,1)} copy(bf16[128,512]{1,0:T(8,128)(2,1)} %shard_map.64) | data formatting | bytes 262144
